TPU v7x, 32 devices: a whole 2x2x4 slice. The times are simulated.
32 devices in a mesh: dp: 8 (over y, x, core), tensor: 4 (over z).
Axes of the slice: x: 2, y: 2, z: 4, core: 2. Of those that a mesh axis runs over, the one named last changes fastest.
Arguments:
- tokens: bfloat16 [4096, 8192], P('dp'), may hold values from -40 to 40
- cotangent: bfloat16 [4096, 2048], P('dp', 'tensor'), may hold values from -260 to 260
- master: float32 [8200, 2048], P('dp', 'tensor'), may hold values from -0.0625 to 0.0625
- first_moment: float32 [8200, 2048], P('dp', 'tensor'), may hold values from -0.0014648438 to 0.0014648438
- second_moment: float32 [8200, 2048], P('dp', 'tensor'), may hold values from 1.7881393e-09 to 1.7881393e-07
- old_rows: int32 [8200], P('dp'), may hold values from 0 to 8199, as said below
Outputs:
- keys_values: bfloat16 [4096, 2048], P('dp', 'tensor')
- update: float32 [8200, 2048], P('dp', 'tensor')
Inputs may be any that keep to these rules, and one draw needn't show every extreme that they name: `old_rows`: every row 0 to 8199 is named by exactly one slot. Rows j * 1025 to (j + 1) * 1025 - 1 belong to new owner j; the slots of one device name at most 257 rows of one owner.
All inputs are finite; a program needn't handle non-finite values.
Results may differ from a plain program's by a relative error of at most 0.0049.
Values may be sent and summed in bfloat16 or wider, within the bound.
A program may use at most 128 MiB of HBM per device.

v0:
```python
import jax
import jax.numpy as jnp
from jax import lax
from jax.sharding import PartitionSpec as P

beta_one = 0.9
beta_two = 0.95
adam_eps = 1e-08
clip_norm = 1.0


def chip_partner(chips, step):
    if chips & (chips - 1) == 0:
        return [c ^ step for c in range(chips)]
    return [(c + step) % chips for c in range(chips)]


def reduce_scatter(partial, rows_dev, peers):
    chips = peers // 2
    me = lax.axis_index("dp")
    core, chip = me % 2, me // 2
    swap = [(d, d ^ 1) for d in range(peers)]
    total = None
    arrived = []
    for step in list(range(chips - 1, 0, -1)) + [0]:
        goes = chip_partner(chips, step)
        target = chip ^ step if chips & (chips - 1) == 0 else (chip + step) % chips
        other = lax.dynamic_slice_in_dim(partial, (2 * target + 1 - core) * rows_dev, rows_dev, 0)
        mine = lax.dynamic_slice_in_dim(partial, (2 * target + core) * rows_dev, rows_dev, 0)
        got = lax.ppermute(other, "dp", swap)
        both = mine.astype(jnp.float32) + got.astype(jnp.float32)
        if step == 0:
            total = both
        else:
            route = [(2 * c + k, 2 * goes[c] + k) for c in range(chips) for k in range(2)]
            arrived.append(lax.ppermute(both.astype(jnp.bfloat16), "dp", route))
    for block in arrived:
        total = total + block.astype(jnp.float32)
    return total


def per_device(tokens, cotangent, master, first_moment, second_moment, old_rows):
    rows_dev = master.shape[0]
    columns_dev = master.shape[1]
    peers = lax.axis_size("dp")
    features = tokens.shape[1]
    all_rows = rows_dev * peers
    capacity = 2 * (rows_dev // peers) + min(rows_dev % peers, 2)
    capacity = -(-capacity // 16) * 16
    owners = old_rows // rows_dev
    targets = old_rows % rows_dev
    chosen = (owners[:, None] == jnp.arange(peers, dtype=jnp.int32)[None, :]).astype(jnp.int32)
    within = jnp.sum((jnp.cumsum(chosen, axis=0) - 1) * chosen, axis=1)
    places = owners * capacity + within
    saved_weight, saved_map = (
        lax.all_gather(master.astype(jnp.bfloat16), "dp", axis=0, tiled=True),
        lax.all_gather(old_rows, "dp", axis=0, tiled=True),
    )

    whole = lax.dot_general(
        tokens, cotangent, (((0,), (0,)), ((), ())), preferred_element_type=jnp.float32
    ).astype(jnp.bfloat16)
    whole = jnp.pad(whole, ((0, all_rows - features), (0, 0)))
    gradient = reduce_scatter(whole, rows_dev, peers)

    box = jnp.arange(peers * capacity, dtype=jnp.int32)
    picks = box[:, None] == places[None, :]
    moments = jnp.concatenate(
        [first_moment.astype(jnp.bfloat16), second_moment.astype(jnp.bfloat16)], axis=1
    )
    outbox = jnp.dot(
        picks.astype(jnp.bfloat16), moments, preferred_element_type=jnp.float32
    ).astype(jnp.bfloat16)
    labels = jnp.max(jnp.where(picks, targets[None, :] + 1, 0), axis=1) - 1
    arrived = lax.all_to_all(
        outbox.reshape(peers, capacity, 2 * columns_dev), "dp", 0, 0, tiled=True
    ).reshape(peers * capacity, 2 * columns_dev)
    arrived_labels = lax.all_to_all(
        labels.reshape(peers, capacity), "dp", 0, 0, tiled=True
    ).reshape(-1)
    puts = jnp.arange(rows_dev, dtype=jnp.int32)[:, None] == arrived_labels[None, :]
    placed = jnp.dot(puts.astype(jnp.bfloat16), arrived, preferred_element_type=jnp.float32)

    weight_full = jnp.zeros((all_rows, columns_dev), jnp.bfloat16).at[saved_map].set(
        saved_weight, unique_indices=True
    )
    product = jnp.dot(tokens, weight_full[:features], preferred_element_type=jnp.float32)
    keys_values = product.astype(jnp.bfloat16)

    squares = lax.psum(jnp.sum(gradient * gradient), ("dp", "tensor"))
    factor = clip_norm / (jnp.sqrt(squares) + 1e-06)
    clipped = gradient * factor
    moment_one = beta_one * placed[:, :columns_dev] + (1.0 - beta_one) * clipped
    moment_two = beta_two * placed[:, columns_dev:] + (1.0 - beta_two) * clipped * clipped
    update = moment_one / (jnp.sqrt(moment_two) + adam_eps)
    return (keys_values, update)


def solution(mesh):
    in_specs = (
        P("dp", None),
        P("dp", "tensor"),
        P("dp", "tensor"),
        P("dp", "tensor"),
        P("dp", "tensor"),
        P("dp"),
    )
    out_specs = (P("dp", "tensor"), P("dp", "tensor"))
    return jax.shard_map(
        per_device, mesh=mesh, in_specs=in_specs, out_specs=out_specs, check_vma=False
    )
```

profile of v0, /device:TPU:0, one launch (start us, length us, event | category | flops | bytes accessed | tf_op | source)
XLA Modules:
  0.0 302.3 jit_solution(16170458503877489241)
XLA Ops:
  7.2 2.9 convert_bitcast_fusion
  10.3 2.3 reduce-window.6
  13.2 1.7 select_reduce_fusion
  15.6 5.2 %all-to-all-start = ((s32[8,1,272]{2,1,0:T(1,128)}), s32[8,1,272]{2,1,0:T(1,128)S(1)}, u32[]{:S(2)}, u32[]{:S(2)}) async-start(s32[8,1,272]{2,1,0:T(1,128)} %sub.35), calls=%async_computation | async-start | bytes 24576 | tf_op jit(solution)/shard_map/all_to_all | solution.py:78
  20.9 1.6 copy-done.3
  22.6 8.8 %fusion.4 = bf16[2176,1024]{1,0:T(8,128)(2,1)} fusion(s32[1025]{0:T(1024)S(1)} %get-tuple-element.20, bf16[1025,512]{1,0:T(8,128)(2,1)S(1)} %convert_element_type.73, bf16[1025,512]{1,0:T(8,128)(2,1)S(1)} %convert_element_type.72), kind=kOutput, calls=%fused_computation.9 | convolution fusion | flops 4576516096 | bytes 6559748 | tf_op jit(solution)/shard_map/dot_general | solution.py:71
  31.4 4.6 %all-to-all-start.1 = ((bf16[8,272,1024]{2,1,0:T(8,128)(2,1)}), bf16[8,272,1024]{2,1,0:T(8,128)(2,1)}, u32[]{:S(2)}, u32[]{:S(2)}) async-start(bf16[8,272,1024]{2,1,0:T(8,128)(2,1)} %bitcast.22), calls=%async_computation.1 | async-start | bytes 8912896 | tf_op jit(solution)/shard_map/all_to_all | solution.py:75
  36.0 10.3 %convolution_convert_fusion = bf16[8192,512]{1,0:T(8,128)(2,1)} fusion(bf16[512,8192]{1,0:T(8,128)(2,1)} %param.6, bf16[512,512]{1,0:T(8,128)(2,1)S(1)} %copy-done), kind=kOutput, calls=%fused_computation.1 | convolution fusion | flops 4299161600 | bytes 17301504 | tf_op jit(solution)/shard_map/dot_general | solution.py:60
  46.3 4.5 %pad_dynamic-slice_fusion.6 = (bf16[1025,512]{1,0:T(8,128)(2,1)S(1)}, bf16[1025,512]{1,0:T(8,128)(2,1)}, bf16[1025,512]{1,0:T(8,128)(2,1)}, bf16[1025,512]{1,0:T(8,128)(2,1)}) fusion(s32[]{:T(128)S(6)} %select_n.60, bf16[8192,512]{1,0:T(8,128)(2,1)} %convolution_convert_fusion, s32[]{:T(128)S(6)} %select_n.62, s32[]{:T(128)S(6)} %select_n.64, s32[]{:T(128)S(6)} %select_n.66), kind=kLoop, calls=%fused_computation.36 | loop fusion | bytes 12587024 | tf_op jit(solution)/shard_map/dynamic_slice | solution.py:28
  51.8 2.0 collective-permute-done.1
  53.8 3.0 collective-permute-done.3
  56.9 2.1 collective-permute-done.5
  58.9 5.3 %add_convert_fusion.2 = (bf16[1025,512]{1,0:T(8,128)(2,1)}, bf16[1025,512]{1,0:T(8,128)(2,1)}, bf16[1025,512]{1,0:T(8,128)(2,1)}) fusion(bf16[1025,512]{1,0:T(8,128)(2,1)} %collective-permute-done.1, s32[]{:T(128)S(6)} %select_n.61, bf16[8192,512]{1,0:T(8,128)(2,1)} %convolution_convert_fusion, bf16[1025,512]{1,0:T(8,128)(2,1)} %collective-permute-done.3, ...), kind=kLoop, calls=%fused_computation.29 | loop fusion | flops 6297600 | bytes 14686220 | tf_op jit(solution)/shard_map/convert_element_type | solution.py:36
  64.2 2.4 collective-permute-start.2
  69.3 103.7 %all-reduce.2 = s32[8200]{0:T(1024)S(1)} all-reduce(s32[8200]{0:T(1024)S(1)} %dynamic-update-slice), channel_id=1, replica_groups=mesh['dp'=8,'tensor'=4] {'dp'}, use_global_device_ids=true, to_apply=%add.2 | all-reduce | flops 8200 | bytes 65600
  173.2 1.0 copy-done.4
  174.1 4.0 %multiply_reduce_fusion = (f32[]{:T(128)}, f32[1025,512]{1,0:T(8,128)S(1)}) fusion(bf16[1025,512]{1,0:T(8,128)(2,1)} %collective-permute-done.6, bf16[1025,512]{1,0:T(8,128)(2,1)} %collective-permute-done.4, bf16[1025,512]{1,0:T(8,128)(2,1)} %collective-permute-done.2, bf16[1025,512]{1,0:T(8,128)(2,1)} %copy-done.4, s32[]{:T(128)S(6)} %select_n.59, ...), kind=kLoop, calls=%fused_computation.25 | loop fusion | flops 5772799 | bytes 14686216 | tf_op jit(solution)/shard_map/reduce_sum | solution.py:90
  178.1 39.8 %psum.7 = f32[]{:T(128)} all-reduce(f32[]{:T(128)} %get-tuple-element.10), channel_id=1, replica_groups=mesh['dp'=8,'tensor'=4] {'dp','tensor'}, use_global_device_ids=true, to_apply=%region_6.7 | all-reduce | flops 1 | bytes 8 | tf_op jit(solution)/shard_map/psum | solution.py:90
  218.6 6.9 %fusion.1 = f32[1025,1024]{1,0:T(8,128)S(1)} fusion(bf16[2176,1024]{1,0:T(8,128)(2,1)} %bitcast.6, s32[2176]{0:T(1024)S(1)} %eq.62), kind=kOutput, calls=%fused_computation.6 | convolution fusion | flops 4570089472 | bytes 8663552 | tf_op jit(solution)/shard_map/dot_general | solution.py:82
  225.6 2.6 fusion.12
  228.1 9.1 %reshape.61 = bf16[8200,512]{1,0:T(8,128)(2,1)} reshape(bf16[8,1025,512]{2,1,0:T(8,128)(2,1)} %all-gather.3.cloned.1.call-done) | data formatting | bytes 16793600
  237.2 46.9 %scatter_custom_fusion = bf16[8200,512]{1,0:T(8,128)(2,1)} fusion(s32[8200]{0:T(1024)S(1)} %compare_select_fusion, bf16[8200,512]{1,0:T(8,128)(2,1)} %reshape.61, bf16[]{:T(256)} %constant.68.clone.1), kind=kCustom, calls=%fused_computation.12 | custom fusion | bytes 8397312 | tf_op jit(solution)/shard_map/scatter | solution.py:84
  284.1 10.4 %fusion.20 = bf16[512,512]{0,1:T(8,128)(2,1)S(1)} fusion(bf16[512,8192]{1,0:T(8,128)(2,1)} %param.6, bf16[8200,512]{1,0:T(8,128)(2,1)} %scatter_custom_fusion), kind=kOutput, calls=%fused_computation.39 | convolution fusion | flops 4295229440 | bytes 17301504 | tf_op jit(solution)/shard_map/dot_general | solution.py:87
  294.4 1.0 copy.14
  (47 shorter events, 4.8 us)
Async XLA Ops:
  7.2 28.8 %copy-start = (bf16[512,512]{1,0:T(8,128)(2,1)S(1)}, bf16[512,512]{1,0:T(8,128)(2,1)}, u32[]{:S(2)}) copy-start(bf16[512,512]{1,0:T(8,128)(2,1)} %param.7) | copy-start | bytes 1572868
  7.2 3.0 copy-start.5
  7.2 13.5 %copy-start.2 = (f32[1025,512]{1,0:T(8,128)S(1)}, f32[1025,512]{1,0:T(8,128)}, u32[]{:S(2)}) copy-start(f32[1025,512]{1,0:T(8,128)} %param.9) | copy-start | bytes 6297604
  7.2 220.9 %all-gather.3.cloned.1.call-start = ((), (), s32[]{:S(2)}) async-start(), calls=%async_computation.2 | async-start | bytes 9510912 | tf_op jit(solution)/shard_map/all_gather | solution.py:56
  15.6 15.9 %all-to-all-start = ((s32[8,1,272]{2,1,0:T(1,128)}), s32[8,1,272]{2,1,0:T(1,128)S(1)}, u32[]{:S(2)}, u32[]{:S(2)}) async-start(s32[8,1,272]{2,1,0:T(1,128)} %sub.35), calls=%async_computation | async-start | bytes 24576 | tf_op jit(solution)/shard_map/all_to_all | solution.py:78
  20.7 1.7 copy-start.3
  31.4 187.2 %all-to-all-start.1 = ((bf16[8,272,1024]{2,1,0:T(8,128)(2,1)}), bf16[8,272,1024]{2,1,0:T(8,128)(2,1)}, u32[]{:S(2)}, u32[]{:S(2)}) async-start(bf16[8,272,1024]{2,1,0:T(8,128)(2,1)} %bitcast.22), calls=%async_computation.1 | async-start | bytes 8912896 | tf_op jit(solution)/shard_map/all_to_all | solution.py:75
  50.8 3.1 %collective-permute-start.1 = (bf16[1025,512]{1,0:T(8,128)(2,1)}, bf16[1025,512]{1,0:T(8,128)(2,1)}, u32[]{:S(2)}, u32[]{:S(2)}) collective-permute-start(bf16[1025,512]{1,0:T(8,128)(2,1)} %get-tuple-element.13), channel_id=1, source_target_pairs={{0,4},{4,0},{8,12},{12,8},{16,20},{20,16},{24,28},{28,24},{1,5},{5... | collective-permute-start | bytes 3148808 | tf_op jit(solution)/shard_map/ppermute | solution.py:30
  51.2 5.7 %collective-permute-start.3 = (bf16[1025,512]{1,0:T(8,128)(2,1)}, bf16[1025,512]{1,0:T(8,128)(2,1)}, u32[]{:S(2)}, u32[]{:S(2)}) collective-permute-start(bf16[1025,512]{1,0:T(8,128)(2,1)} %get-tuple-element.14), channel_id=1, source_target_pairs={{0,4},{4,0},{8,12},{12,8},{16,20},{20,16},{24,28},{28,24},{1,5},{5... | collective-permute-start | bytes 3148808 | tf_op jit(solution)/shard_map/ppermute | solution.py:30
  51.3 7.7 %collective-permute-start.5 = (bf16[1025,512]{1,0:T(8,128)(2,1)}, bf16[1025,512]{1,0:T(8,128)(2,1)}, u32[]{:S(2)}, u32[]{:S(2)}) collective-permute-start(bf16[1025,512]{1,0:T(8,128)(2,1)} %get-tuple-element.15), channel_id=1, source_target_pairs={{0,4},{4,0},{8,12},{12,8},{16,20},{20,16},{24,28},{28,24},{1,5},{5... | collective-permute-start | bytes 3148808 | tf_op jit(solution)/shard_map/ppermute | solution.py:30
  51.7 121.4 %collective-permute-start = (bf16[1025,512]{1,0:T(8,128)(2,1)S(1)}, bf16[1025,512]{1,0:T(8,128)(2,1)S(1)}, u32[]{:S(2)}, u32[]{:S(2)}) collective-permute-start(bf16[1025,512]{1,0:T(8,128)(2,1)S(1)} %get-tuple-element.12), channel_id=1, source_target_pairs={{0,4},{4,0},{8,12},{12,8},{16,20},{20,16},{24,28},{28,24},{1,5},{5... | collective-permute-start | bytes 3148808 | tf_op jit(solution)/shard_map/ppermute | solution.py:30
  51.8 15.9 %copy-start.6 = (u32[32]{0:T(128)S(1)}, u32[32]{0:T(128)}, u32[]{:S(2)}) copy-start(u32[32]{0:T(128)} %constant.99) | copy-start | bytes 388
  64.2 108.9 %collective-permute-start.2 = (bf16[1025,512]{1,0:T(8,128)(2,1)}, bf16[1025,512]{1,0:T(8,128)(2,1)}, u32[]{:S(2)}, u32[]{:S(2)}) collective-permute-start(bf16[1025,512]{1,0:T(8,128)(2,1)} %get-tuple-element.16), channel_id=1, source_target_pairs={{0,24},{4,28},{8,16},{12,20},{16,8},{20,12},{24,0},{28,4},{1,25},{... | collective-permute-start | bytes 3148808 | tf_op jit(solution)/shard_map/ppermute | solution.py:36
  66.6 106.5 %collective-permute-start.4 = (bf16[1025,512]{1,0:T(8,128)(2,1)}, bf16[1025,512]{1,0:T(8,128)(2,1)}, u32[]{:S(2)}, u32[]{:S(2)}) collective-permute-start(bf16[1025,512]{1,0:T(8,128)(2,1)} %get-tuple-element.17), channel_id=1, source_target_pairs={{0,16},{4,20},{8,24},{12,28},{16,0},{20,4},{24,8},{28,12},{1,17},{... | collective-permute-start | bytes 3148808 | tf_op jit(solution)/shard_map/ppermute | solution.py:36
  67.2 106.9 %collective-permute-start.6 = (bf16[1025,512]{1,0:T(8,128)(2,1)}, bf16[1025,512]{1,0:T(8,128)(2,1)}, u32[]{:S(2)}, u32[]{:S(2)}) collective-permute-start(bf16[1025,512]{1,0:T(8,128)(2,1)} %get-tuple-element.18), channel_id=1, source_target_pairs={{0,8},{4,12},{8,0},{12,4},{16,24},{20,28},{24,16},{28,20},{1,9},{5... | collective-permute-start | bytes 3148808 | tf_op jit(solution)/shard_map/ppermute | solution.py:36
  173.1 1.0 copy-start.4
  284.1 11.4 %copy-start.1 = (bf16[512,512]{1,0:T(8,128)(2,1)S(1)}, bf16[512,512]{1,0:T(8,128)(2,1)}, u32[]{:S(2)}) copy-start(bf16[512,512]{1,0:T(8,128)(2,1)} %param.7) | copy-start | bytes 1572868
Sparse Core Ops, SparseCore 0:
  10.3 126.7 all-gather.2
where the time goes:
time: 303 us; the launch traced here: 302 us
  blocking collectives  143 us (47%)
  local copies, waits for them, and re-layouts  66 us (22%)
  matrix products  36.4 us (12%)
  other arithmetic  19.4 us (6%)
  between operations  15.7 us (5%)
  starting transfers between devices  14.3 us (5%)
  waiting for transfers between devices  7.18 us (2%)
    unnamed x1, blocking collectives  104 us
    scatter x1, local copies, waits for them, and re-layouts, per_device(): jnp.zeros((all_rows, columns_dev), jnp.bfloat16).at[saved_map]  46.9 us
    psum x1, blocking collectives, per_device(): squares = lax.psum(jnp.sum(gradient * gradient), ('dp', 'tensor'))  39.8 us
    unnamed x20, local copies, waits for them, and re-layouts  13.6 us
    dot_general x1, matrix products, per_device(): jnp.dot(tokens, weight_full[:features], preferred_element_type=jnp.float32)  10.4 us
    dot_general x1, matrix products, per_device(): lax.dot_general(tokens, cotangent, (((0,), (0,)), ((), ())), preferred_el...  10.3 us
    dot_general x1, matrix products, per_device(): jnp.dot(picks.astype(jnp.bfloat16), moments, preferred_element_type=jnp.f...  8.82 us
    ppermute x4, waiting for transfers between devices, reduce_scatter(): got = lax.ppermute(other, 'dp', swap)  7.15 us
  transfers between devices with their start and end apart: 10, of which 3 were waited for; matrix products, arithmetic and copies ran while one was open for 16% of the time, Pallas kernels for 0%

commit v1 on v0

v1 whole, which is shorter than its diff:
```python
import functools

import jax
import jax.numpy as jnp
from jax import lax
from jax.experimental import pallas as pl
from jax.experimental.pallas import tpu as pltpu
from jax.sharding import PartitionSpec as P

beta_one = 0.9
beta_two = 0.95
adam_eps = 1e-08
clip_norm = 1.0


def chip_partner(chips, step):
    if chips & (chips - 1) == 0:
        return [c ^ step for c in range(chips)]
    return [(c + step) % chips for c in range(chips)]


def sum_kernel(peers, groups, x_ref, o_ref, part, from_dp, from_tensor, send_dp, recv_dp, send_t, recv_t):
    row = lax.axis_index("dp")
    column = lax.axis_index("tensor")
    rows = [lax.rem(row + s, peers) for s in range(1, peers)]
    columns = [lax.rem(column + s, groups) for s in range(1, groups)]
    everyone = [(r, column) for r in rows] + [(row, c) for c in columns]
    barrier = pltpu.get_barrier_semaphore()
    for device in everyone:
        pl.semaphore_signal(barrier, inc=1, device_id=device, device_id_type=pl.DeviceIdType.MESH)
    pl.semaphore_wait(barrier, len(everyone))

    def exchange(source, slots, send, recv, devices):
        copies = [
            pltpu.make_async_remote_copy(
                src_ref=source,
                dst_ref=slots.at[k],
                send_sem=send.at[k],
                recv_sem=recv.at[k],
                device_id=device,
                device_id_type=pl.DeviceIdType.MESH,
            )
            for k, device in enumerate(devices)
        ]
        for copy in copies:
            copy.start()
        for copy in copies:
            copy.wait()
        total = source[...]
        for k in range(len(devices)):
            total = total + slots[k]
        return total

    part[...] = exchange(x_ref, from_dp, send_dp, recv_dp, [(r, column) for r in rows])
    o_ref[...] = exchange(part, from_tensor, send_t, recv_t, [(row, c) for c in columns])


def sum_over_mesh(value):
    peers, groups = lax.axis_size("dp"), lax.axis_size("tensor")
    tile = (8, 128)
    return pl.pallas_call(
        functools.partial(sum_kernel, peers, groups),
        out_shape=jax.ShapeDtypeStruct(tile, jnp.float32),
        in_specs=[pl.BlockSpec(memory_space=pltpu.VMEM)],
        out_specs=pl.BlockSpec(memory_space=pltpu.VMEM),
        scratch_shapes=[
            pltpu.VMEM(tile, jnp.float32),
            pltpu.VMEM((peers - 1,) + tile, jnp.float32),
            pltpu.VMEM((groups - 1,) + tile, jnp.float32),
            pltpu.SemaphoreType.DMA((peers - 1,)),
            pltpu.SemaphoreType.DMA((peers - 1,)),
            pltpu.SemaphoreType.DMA((groups - 1,)),
            pltpu.SemaphoreType.DMA((groups - 1,)),
        ],
        compiler_params=pltpu.CompilerParams(collective_id=0, has_side_effects=True),
    )(jnp.full(tile, value, jnp.float32))[0, 0]


def sum_cores(partial, rows_dev, peers):
    chips = peers // 2
    me = lax.axis_index("dp")
    core, chip = me % 2, me // 2
    swap = [(d, d ^ 1) for d in range(peers)]
    sums = []
    for step in range(chips):
        target = chip ^ step if chips & (chips - 1) == 0 else (chip + step) % chips
        other = lax.dynamic_slice_in_dim(partial, (2 * target + 1 - core) * rows_dev, rows_dev, 0)
        mine = lax.dynamic_slice_in_dim(partial, (2 * target + core) * rows_dev, rows_dev, 0)
        got = lax.ppermute(other, "dp", swap)
        both = mine.astype(jnp.float32) + got.astype(jnp.float32)
        sums.append(both if step == 0 else both.astype(jnp.bfloat16))
    return sums


def sum_chips(own, blocks, peers):
    chips = peers // 2
    arrived = []
    for step, block in reversed(list(enumerate(blocks, 1))):
        goes = chip_partner(chips, step)
        route = [(2 * c + k, 2 * goes[c] + k) for c in range(chips) for k in range(2)]
        arrived.append(lax.ppermute(block, "dp", route))
    for block in arrived:
        own = own + block.astype(jnp.float32)
    return own


def per_device(tokens, cotangent, master, first_moment, second_moment, old_rows):
    rows_dev = master.shape[0]
    columns_dev = master.shape[1]
    peers = lax.axis_size("dp")
    features = tokens.shape[1]
    all_rows = rows_dev * peers
    capacity = 2 * (rows_dev // peers) + min(rows_dev % peers, 2)
    capacity = -(-capacity // 16) * 16
    owners = old_rows // rows_dev
    targets = old_rows % rows_dev
    chosen = (owners[:, None] == jnp.arange(peers, dtype=jnp.int32)[None, :]).astype(jnp.int32)
    within = jnp.sum((jnp.cumsum(chosen, axis=0) - 1) * chosen, axis=1)
    places = owners * capacity + within

    box = jnp.arange(peers * capacity, dtype=jnp.int32)
    picks = box[:, None] == places[None, :]
    labels = jnp.max(jnp.where(picks, targets[None, :] + 1, 0), axis=1) - 1
    notes = jnp.concatenate(
        [
            labels.reshape(peers, 1, capacity),
            jnp.broadcast_to(old_rows[None, None, :], (peers, 1, rows_dev)),
        ],
        axis=2,
    )
    notes = lax.all_to_all(notes, "dp", 0, 0, tiled=True)
    arrived_labels = notes[:, 0, :capacity].reshape(-1)
    saved_map = notes[:, 0, capacity:].reshape(-1)
    saved_weight = lax.all_gather(master.astype(jnp.bfloat16), "dp", axis=0, tiled=True)

    whole = lax.dot_general(
        tokens, cotangent, (((0,), (0,)), ((), ())), preferred_element_type=jnp.float32
    ).astype(jnp.bfloat16)
    whole = jnp.pad(whole, ((0, all_rows - features), (0, 0)))
    own, *blocks = sum_cores(whole, rows_dev, peers)
    moments = jnp.concatenate(
        [first_moment.astype(jnp.bfloat16), second_moment.astype(jnp.bfloat16)], axis=1
    )
    outbox = jnp.dot(
        picks.astype(jnp.bfloat16), moments, preferred_element_type=jnp.float32
    ).astype(jnp.bfloat16)
    saved_weight, outbox, blocks = lax.optimization_barrier((saved_weight, outbox, blocks))
    gradient = sum_chips(own, blocks, peers)
    arrived = lax.all_to_all(
        outbox.reshape(peers, capacity, 2 * columns_dev), "dp", 0, 0, tiled=True
    ).reshape(peers * capacity, 2 * columns_dev)
    puts = jnp.arange(rows_dev, dtype=jnp.int32)[:, None] == arrived_labels[None, :]
    placed = jnp.dot(puts.astype(jnp.bfloat16), arrived, preferred_element_type=jnp.float32)

    weight_full = jnp.zeros((all_rows, columns_dev), jnp.bfloat16).at[saved_map].set(
        saved_weight, unique_indices=True
    )
    product = jnp.dot(tokens, weight_full[:features], preferred_element_type=jnp.float32)
    keys_values = product.astype(jnp.bfloat16)

    local, keys_values = lax.optimization_barrier((jnp.sum(gradient * gradient), keys_values))
    squares = sum_over_mesh(local)
    factor = clip_norm / (jnp.sqrt(squares) + 1e-06)
    clipped = gradient * factor
    moment_one = beta_one * placed[:, :columns_dev] + (1.0 - beta_one) * clipped
    moment_two = beta_two * placed[:, columns_dev:] + (1.0 - beta_two) * clipped * clipped
    update = moment_one / (jnp.sqrt(moment_two) + adam_eps)
    return (keys_values, update)


def solution(mesh):
    in_specs = (
        P("dp", None),
        P("dp", "tensor"),
        P("dp", "tensor"),
        P("dp", "tensor"),
        P("dp", "tensor"),
        P("dp"),
    )
    out_specs = (P("dp", "tensor"), P("dp", "tensor"))
    return jax.shard_map(
        per_device, mesh=mesh, in_specs=in_specs, out_specs=out_specs, check_vma=False
    )
```

time: 303 us -> 215 us (0.71)
  blocking collectives: 143 us -> 0 us
  waiting for transfers between devices: 7.18 us -> 51.3 us
  Pallas kernels: 0 us -> 10.9 us
    unnamed x1 -> x0, blocking collectives: 104 us -> none
    psum x1 -> x0, blocking collectives: 39.8 us -> none  [per_device(): squares = lax.psum(jnp.sum(gradient * gradient), ('dp', 'tensor'))]
    ppermute x7, waiting for transfers between devices: 7.16 us -> 35.5 us  [the longest x3 35.5 us: sum_chips(): arrived.append(lax.ppermute(block, 'dp', route))]
    all_gather x1, waiting for transfers between devices: 0.01 us -> 15.7 us  [per_device(): lax.all_gather(master.astype(jnp.bfloat16), 'dp', axis=0, tiled=True)]
    pallas_call x0 -> x1, Pallas kernels: none -> 10.9 us  [sum_over_mesh(): pl.pallas_call(functools.partial(sum_kernel, peers, groups), out_shape=ja...]
    optimization_barrier x0 -> x1, local copies, waits for them, and re-layouts: none -> 9.07 us  [per_device(): lax.optimization_barrier((saved_weight, outbox, blocks))]
    unnamed x20, local copies, waits for them, and re-layouts: 13.6 us -> 5.72 us
  transfers between devices with their start and end apart: 10 -> 10, of which waited for: 3 -> 3; matrix products, arithmetic and copies ran while one was open for 16% -> 49% of each run, Pallas kernels for 0% -> 5%
where the time goes in v1:
time: 215 us
  local copies, waits for them, and re-layouts  67.6 us (31%)
  waiting for transfers between devices  51.3 us (24%)
  matrix products  34.2 us (16%)
  other arithmetic  21.1 us (10%)
  between operations  15.1 us (7%)
  starting transfers between devices  14.4 us (7%)
  Pallas kernels  10.9 us (5%)
    scatter x1, local copies, waits for them, and re-layouts, per_device(): jnp.zeros((all_rows, columns_dev), jnp.bfloat16).at[saved_map]  46.9 us
    ppermute x3, waiting for transfers between devices, sum_chips(): arrived.append(lax.ppermute(block, 'dp', route))  35.5 us
    all_gather x1, waiting for transfers between devices, per_device(): lax.all_gather(master.astype(jnp.bfloat16), 'dp', axis=0, tiled=True)  15.7 us
    pallas_call x1, Pallas kernels, sum_over_mesh(): pl.pallas_call(functools.partial(sum_kernel, peers, groups), out_shape=ja...  10.9 us
    dot_general x1, matrix products, per_device(): jnp.dot(tokens, weight_full[:features], preferred_element_type=jnp.float32)  10.3 us
    optimization_barrier x1, local copies, waits for them, and re-layouts, per_device(): lax.optimization_barrier((saved_weight, outbox, blocks))  9.07 us
    dot_general x1, matrix products, per_device(): jnp.dot(picks.astype(jnp.bfloat16), moments, preferred_element_type=jnp.f...  8.74 us
    dot_general x1, matrix products, per_device(): lax.dot_general(tokens, cotangent, (((0,), (0,)), ((), ())), preferred_el...  8.25 us
  transfers between devices with their start and end apart: 10, of which 3 were waited for; matrix products, arithmetic and copies ran while one was open for 49% of the time, Pallas kernels for 5%

profile of v1, /device:TPU:0, one launch (start us, length us, event | category | flops | bytes accessed | tf_op | source)
XLA Modules:
  0.0 214.6 jit_solution(9102598176806936402)
XLA Ops:
  7.2 2.8 %convert_bitcast_fusion = bf16[1,1025,512]{2,1,0:T(8,128)(2,1)} fusion(f32[1025,512]{1,0:T(8,128)} %param.8), kind=kLoop, calls=%fused_computation.40 | loop fusion | flops 524800 | bytes 3148800
  10.1 8.2 %convolution_convert_fusion = bf16[8192,512]{1,0:T(8,128)(2,1)S(1)} fusion(bf16[512,8192]{1,0:T(8,128)(2,1)} %param.6, bf16[512,512]{1,0:T(8,128)(2,1)S(1)} %copy-done), kind=kOutput, calls=%fused_computation.1 | convolution fusion | flops 4299161600 | bytes 17301504 | tf_op jit(solution)/shard_map/dot_general | solution.py:136
  18.4 2.6 %pad_dynamic-slice_fusion.6 = (bf16[1025,512]{1,0:T(8,128)(2,1)}, bf16[1025,512]{1,0:T(8,128)(2,1)}, bf16[1025,512]{1,0:T(8,128)(2,1)}, bf16[1025,512]{1,0:T(8,128)(2,1)}) fusion(s32[]{:T(128)S(6)} %select_n.63, bf16[8192,512]{1,0:T(8,128)(2,1)S(1)} %convolution_convert_fusion, s32[]{:T(128)S(6)} %select_n.66, s32[]{:T(128)S(6)} %select_n.68, s32[]{:T(128)S(6)} %select_n.70), kind=kLoop, calls=%fused_computation.36 | loop fusion | bytes 12587024 | tf_op jit(solution)/shard_map/dynamic_slice | solution.py:87
  21.0 2.8 %copy-done.2 = bf16[8192,512]{1,0:T(8,128)(2,1)} copy-done((bf16[8192,512]{1,0:T(8,128)(2,1)}, bf16[8192,512]{1,0:T(8,128)(2,1)S(1)}, u32[]{:S(2)}) %copy-start.2) | copy-done | bytes 8388632
  24.8 2.3 %reduce-window.6 = s32[8,9,128]{2,1,0:T(8,128)S(1)} reduce-window(s32[8,9,128]{2,1,0:T(8,128)S(1)} %copy.13, s32[]{:T(128)} %constant.74.clone.1), window={size=1x1x128 pad=0_0x0_0x127_0}, to_apply=%region_0.1 | reduce-window | flops 1170432 | bytes 73732 | tf_op jit(solution)/shard_map/reduce-window
  27.7 1.7 select_reduce_fusion
  30.2 4.7 %all-to-all-start = ((s32[8,1,1297]{2,1,0:T(1,128)}), s32[8,1,1297]{2,1,0:T(1,128)S(1)}, u32[]{:S(2)}, u32[]{:S(2)}) async-start(s32[8,1,1297]{2,1,0:T(1,128)} %pad_add_fusion), calls=%async_computation | async-start | bytes 90112 | tf_op jit(solution)/shard_map/all_to_all | solution.py:131
  38.1 8.7 %fusion.4 = bf16[2176,1024]{1,0:T(8,128)(2,1)} fusion(s32[1025]{0:T(1024)S(1)} %get-tuple-element.34, bf16[1025,512]{1,0:T(8,128)(2,1)S(1)} %copy-done.7, bf16[1025,512]{1,0:T(8,128)(2,1)S(1)} %convert_element_type.73), kind=kOutput, calls=%fused_computation.9 | convolution fusion | flops 4576516096 | bytes 6559748 | tf_op jit(solution)/shard_map/dot_general | solution.py:144
  46.8 5.3 %add_convert_fusion = (bf16[1025,512]{1,0:T(8,128)(2,1)}, bf16[1025,512]{1,0:T(8,128)(2,1)}, bf16[1025,512]{1,0:T(8,128)(2,1)}) fusion(bf16[1025,512]{1,0:T(8,128)(2,1)} %collective-permute-done.3, s32[]{:T(128)S(6)} %select_n.69, bf16[8192,512]{1,0:T(8,128)(2,1)} %copy-done.2, bf16[1025,512]{1,0:T(8,128)(2,1)} %collective-permute-done.1, s32[]{:T(128)S(6)} %select_n.65, ...), kind=kLoop, calls=%fused_computation.27 | loop fusion | flops 6297600 | bytes 14686220 | tf_op jit(solution)/shard_map/convert_element_type | solution.py:91
  52.1 15.7 %all-gather.3.cloned.1.call-done = bf16[8,1025,512]{2,1,0:T(8,128)(2,1)} async-done(((bf16[1,1025,512]{2,1,0:T(8,128)(2,1)}), bf16[8,1025,512]{2,1,0:T(8,128)(2,1)}) %all-gather.3.cloned.1.call-update) | async-done | bytes 8396816 | tf_op jit(solution)/shard_map/all_gather | solution.py:134
  67.9 9.1 %reshape.89 = bf16[8200,512]{1,0:T(8,128)(2,1)} reshape(bf16[8,1025,512]{2,1,0:T(8,128)(2,1)} %all-gather.3.cloned.1.call-done) | data formatting | bytes 16793600 | tf_op jit(solution)/shard_map/optimization_barrier | solution.py:147
  76.9 5.0 %all-to-all-start.1 = ((bf16[8,272,1024]{2,1,0:T(8,128)(2,1)}), bf16[8,272,1024]{2,1,0:T(8,128)(2,1)}, u32[]{:S(2)}, u32[]{:S(2)}) async-start(bf16[8,272,1024]{2,1,0:T(8,128)(2,1)} %bitcast.22), calls=%async_computation.1 | async-start | bytes 8912896 | tf_op jit(solution)/shard_map/all_to_all | solution.py:149
  82.7 1.7 collective-permute-start.6
  84.4 1.5 collective-permute-start.5
  86.2 46.9 %scatter_custom_fusion = bf16[8200,512]{1,0:T(8,128)(2,1)} fusion(s32[8200]{0:T(1024)S(1)} %fusion.25, bf16[8200,512]{1,0:T(8,128)(2,1)} %reshape.89, bf16[]{:T(256)} %constant.70.clone.1), kind=kCustom, calls=%fused_computation.12 | custom fusion | bytes 8397312 | tf_op jit(solution)/shard_map/scatter | solution.py:155
  133.1 10.3 %fusion.20 = bf16[512,512]{0,1:T(8,128)(2,1)S(1)} fusion(bf16[512,8192]{1,0:T(8,128)(2,1)} %param.6, bf16[8200,512]{1,0:T(8,128)(2,1)} %scatter_custom_fusion), kind=kOutput, calls=%fused_computation.39 | convolution fusion | flops 4295229440 | bytes 17301504 | tf_op jit(solution)/shard_map/dot_general | solution.py:158
  143.4 12.4 %collective-permute-done.6 = bf16[1025,512]{1,0:T(8,128)(2,1)} collective-permute-done((bf16[1025,512]{1,0:T(8,128)(2,1)}, bf16[1025,512]{1,0:T(8,128)(2,1)}, u32[]{:S(2)}, u32[]{:S(2)}) %collective-permute-start.6) | collective-permute-done | bytes 1049632 | tf_op jit(solution)/shard_map/ppermute | solution.py:101
  155.9 23.1 %collective-permute-done.4 = bf16[1025,512]{1,0:T(8,128)(2,1)} collective-permute-done((bf16[1025,512]{1,0:T(8,128)(2,1)}, bf16[1025,512]{1,0:T(8,128)(2,1)}, u32[]{:S(2)}, u32[]{:S(2)}) %collective-permute-start.4) | collective-permute-done | bytes 1049632 | tf_op jit(solution)/shard_map/ppermute | solution.py:101
  179.0 4.1 %multiply_reduce_fusion = (f32[]{:T(128)}, f32[1025,512]{1,0:T(8,128)S(1)}) fusion(bf16[1025,512]{1,0:T(8,128)(2,1)} %collective-permute-done.6, bf16[1025,512]{1,0:T(8,128)(2,1)} %collective-permute-done.5, bf16[1025,512]{1,0:T(8,128)(2,1)} %collective-permute-done.4, bf16[1025,512]{1,0:T(8,128)(2,1)} %copy-done.6, s32[]{:T(128)S(6)} %select_n.62, ...), kind=kLoop, calls=%fused_computation.25 | loop fusion | flops 5772799 | bytes 14686216 | tf_op jit(solution)/shard_map/reduce_sum | solution.py:161
  184.1 1.3 broadcast_in_dim.35.x_ref
  185.4 10.9 %shard_map.77 = f32[8,128]{1,0:T(8,128)} custom-call(f32[8,128]{1,0:T(8,128)} %broadcast_in_dim.35.x_ref), custom_call_target="tpu_custom_call" | custom-call | tf_op jit(solution)/shard_map/pallas_call | solution.py:61
  196.3 1.2 slice.34
  198.2 6.9 %fusion.1 = f32[1025,1024]{1,0:T(8,128)S(1)} fusion(bf16[2176,1024]{1,0:T(8,128)(2,1)} %bitcast.5, s32[2176]{0:T(1024)S(1)} %eq.62), kind=kOutput, calls=%fused_computation.6 | convolution fusion | flops 4570089472 | bytes 8663552 | tf_op jit(solution)/shard_map/dot_general | solution.py:153
  205.2 2.6 %fusion.12 = f32[1025,512]{1,0:T(8,128)} fusion(f32[1025,1024]{1,0:T(8,128)S(1)} %fusion.1, f32[1025,512]{1,0:T(8,128)S(1)} %get-tuple-element.25, f32[]{:T(128)} %bitcast.6), kind=kLoop, calls=%fused_computation.18 | loop fusion | flops 5248000 | bytes 8396804 | tf_op jit(solution)/shard_map/div | solution.py:167
  (53 shorter events, 7.7 us)
Async XLA Ops:
  7.2 2.9 %copy-start = (bf16[512,512]{1,0:T(8,128)(2,1)S(1)}, bf16[512,512]{1,0:T(8,128)(2,1)}, u32[]{:S(2)}) copy-start(bf16[512,512]{1,0:T(8,128)(2,1)} %param.7) | copy-start | bytes 1572868
  7.2 60.7 %all-gather.3.cloned.1.call-start = ((), (), s32[]{:S(2)}) async-start(), calls=%async_computation.2 | async-start | bytes 9510912 | tf_op jit(solution)/shard_map/all_gather | solution.py:134
  18.3 5.4 %copy-start.2 = (bf16[8192,512]{1,0:T(8,128)(2,1)}, bf16[8192,512]{1,0:T(8,128)(2,1)S(1)}, u32[]{:S(2)}) copy-start(bf16[8192,512]{1,0:T(8,128)(2,1)S(1)} %convolution_convert_fusion) | copy-start | bytes 25165828
  18.3 6.4 %copy-start.8 = (s32[1025]{0:T(1024)S(1)}, s32[1025]{0:T(1024)}, u32[]{:S(2)}) copy-start(s32[1025]{0:T(1024)} %param.11) | copy-start | bytes 12304
  18.3 16.5 %copy-start.3 = (f32[1025,512]{1,0:T(8,128)S(1)}, f32[1025,512]{1,0:T(8,128)}, u32[]{:S(2)}) copy-start(f32[1025,512]{1,0:T(8,128)} %param.10) | copy-start | bytes 6297604
  23.8 23.0 %collective-permute-start.3 = (bf16[1025,512]{1,0:T(8,128)(2,1)}, bf16[1025,512]{1,0:T(8,128)(2,1)}, u32[]{:S(2)}, u32[]{:S(2)}) collective-permute-start(bf16[1025,512]{1,0:T(8,128)(2,1)} %get-tuple-element.29), channel_id=1, source_target_pairs={{0,4},{4,0},{8,12},{12,8},{16,20},{20,16},{24,28},{28,24},{1,5},{5... | collective-permute-start | bytes 3148808 | tf_op jit(solution)/shard_map/ppermute | solution.py:89
  24.2 22.6 %collective-permute-start.1 = (bf16[1025,512]{1,0:T(8,128)(2,1)}, bf16[1025,512]{1,0:T(8,128)(2,1)}, u32[]{:S(2)}, u32[]{:S(2)}) collective-permute-start(bf16[1025,512]{1,0:T(8,128)(2,1)} %get-tuple-element.27), channel_id=1, source_target_pairs={{0,4},{4,0},{8,12},{12,8},{16,20},{20,16},{24,28},{28,24},{1,5},{5... | collective-permute-start | bytes 3148808 | tf_op jit(solution)/shard_map/ppermute | solution.py:89
  24.3 22.5 %collective-permute-start.2 = (bf16[1025,512]{1,0:T(8,128)(2,1)}, bf16[1025,512]{1,0:T(8,128)(2,1)}, u32[]{:S(2)}, u32[]{:S(2)}) collective-permute-start(bf16[1025,512]{1,0:T(8,128)(2,1)} %get-tuple-element.28), channel_id=1, source_target_pairs={{0,4},{4,0},{8,12},{12,8},{16,20},{20,16},{24,28},{28,24},{1,5},{5... | collective-permute-start | bytes 3148808 | tf_op jit(solution)/shard_map/ppermute | solution.py:89
  30.2 46.8 %all-to-all-start = ((s32[8,1,1297]{2,1,0:T(1,128)}), s32[8,1,1297]{2,1,0:T(1,128)S(1)}, u32[]{:S(2)}, u32[]{:S(2)}) async-start(s32[8,1,1297]{2,1,0:T(1,128)} %pad_add_fusion), calls=%async_computation | async-start | bytes 90112 | tf_op jit(solution)/shard_map/all_to_all | solution.py:131
  34.9 2.0 copy-start.4
  36.8 1.2 copy-start.7
  76.9 5.0 %copy-start.5 = (bf16[1025,512]{1,0:T(8,128)(2,1)S(1)}, bf16[1025,512]{1,0:T(8,128)(2,1)}, u32[]{:S(2)}) copy-start(bf16[1025,512]{1,0:T(8,128)(2,1)} %get-tuple-element.26) | copy-start | bytes 3148804
  76.9 121.3 %all-to-all-start.1 = ((bf16[8,272,1024]{2,1,0:T(8,128)(2,1)}), bf16[8,272,1024]{2,1,0:T(8,128)(2,1)}, u32[]{:S(2)}, u32[]{:S(2)}) async-start(bf16[8,272,1024]{2,1,0:T(8,128)(2,1)} %bitcast.22), calls=%async_computation.1 | async-start | bytes 8912896 | tf_op jit(solution)/shard_map/all_to_all | solution.py:149
  82.0 61.5 %collective-permute-start = (bf16[1025,512]{1,0:T(8,128)(2,1)S(1)}, bf16[1025,512]{1,0:T(8,128)(2,1)S(1)}, u32[]{:S(2)}, u32[]{:S(2)}) collective-permute-start(bf16[1025,512]{1,0:T(8,128)(2,1)S(1)} %copy-done.5), channel_id=1, source_target_pairs={{0,4},{4,0},{8,12},{12,8},{16,20},{20,16},{24,28},{28,24},{1,5},{5... | collective-permute-start | bytes 3148808 | tf_op jit(solution)/shard_map/ppermute | solution.py:89
  82.7 73.2 %collective-permute-start.6 = (bf16[1025,512]{1,0:T(8,128)(2,1)}, bf16[1025,512]{1,0:T(8,128)(2,1)}, u32[]{:S(2)}, u32[]{:S(2)}) collective-permute-start(bf16[1025,512]{1,0:T(8,128)(2,1)} %get-tuple-element.11), channel_id=1, source_target_pairs={{0,8},{4,12},{8,0},{12,4},{16,24},{20,28},{24,16},{28,20},{1,9},{5... | collective-permute-start | bytes 3148808 | tf_op jit(solution)/shard_map/ppermute | solution.py:101
  84.4 71.5 %collective-permute-start.5 = (bf16[1025,512]{1,0:T(8,128)(2,1)}, bf16[1025,512]{1,0:T(8,128)(2,1)}, u32[]{:S(2)}, u32[]{:S(2)}) collective-permute-start(bf16[1025,512]{1,0:T(8,128)(2,1)} %get-tuple-element.10), channel_id=1, source_target_pairs={{0,16},{4,20},{8,24},{12,28},{16,0},{20,4},{24,8},{28,12},{1,17},{... | collective-permute-start | bytes 3148808 | tf_op jit(solution)/shard_map/ppermute | solution.py:101
  85.9 93.1 %collective-permute-start.4 = (bf16[1025,512]{1,0:T(8,128)(2,1)}, bf16[1025,512]{1,0:T(8,128)(2,1)}, u32[]{:S(2)}, u32[]{:S(2)}) collective-permute-start(bf16[1025,512]{1,0:T(8,128)(2,1)} %get-tuple-element.9), channel_id=1, source_target_pairs={{0,24},{4,28},{8,16},{12,20},{16,8},{20,12},{24,0},{28,4},{1,25},{... | collective-permute-start | bytes 3148808 | tf_op jit(solution)/shard_map/ppermute | solution.py:101
  143.4 12.5 %copy-start.6 = (bf16[1025,512]{1,0:T(8,128)(2,1)}, bf16[1025,512]{1,0:T(8,128)(2,1)S(1)}, u32[]{:S(2)}) copy-start(bf16[1025,512]{1,0:T(8,128)(2,1)S(1)} %collective-permute-done) | copy-start | bytes 3148804
  205.1 2.6 %copy-start.1 = (bf16[512,512]{1,0:T(8,128)(2,1)S(1)}, bf16[512,512]{1,0:T(8,128)(2,1)}, u32[]{:S(2)}) copy-start(bf16[512,512]{1,0:T(8,128)(2,1)} %param.7) | copy-start | bytes 1572868
Sparse Core Ops, SparseCore 0:
  10.5 57.3 all-gather.2
